TPU v7x, 32 devices: a whole 2x2x4 slice. The times are simulated.
32 devices in a mesh: groups: 2 (over y), space: 16 (over z, x, core).
Axes of the slice: x: 2, y: 2, z: 4, core: 2. Of those that a mesh axis runs over, the one named last changes fastest.
Arguments:
- video: bfloat16 [64, 16, 256, 256], P(None, None, ('groups', 'space')), parts along dimension 2, may hold values from -16 to 16
- shrink: float32 [2], P('groups'), parts along dimension 0, may hold values from 0.1 to 1
Outputs:
- denoised: bfloat16 [64, 16, 256, 256], P(None, None, ('groups', 'space')), parts along dimension 2
There are 2 independent parts, one for each index of `groups`. A program takes and returns all parts, laid end to end along the dimension named above; each array names one. Nothing has to cross between parts.
All inputs are finite; a program needn't handle non-finite values.
Results may differ from a plain program's by a relative error of at most 0.001.
The roundings to bfloat16 on the way count: a program that leaves them out, or rounds other values in their place, can miss the bound.
Values may be sent and summed in bfloat16 or wider, within the bound.
A program may use at most 128 MiB of HBM per device.

v0:
```python
import jax
import jax.numpy as jnp
from jax import lax
from jax.sharding import PartitionSpec as P


def padded_2(shard, sides, width):
    for axis, dim in sides:
        devices, length = (lax.axis_size(axis), shard.shape[dim])
        up = [(i, (i + 1) % devices) for i in range(devices - 1)]
        down = [(j, i) for i, j in up]
        last = lax.slice_in_dim(shard, length - width, length, axis=dim)
        first = lax.slice_in_dim(shard, 0, width, axis=dim)
        before = lax.ppermute(last, axis, up)
        after = lax.ppermute(first, axis, down)
        shard = jnp.concatenate([before, shard, after], axis=dim)
    return shard


def smooth_local(field, axis):
    count = field.shape[axis]
    widths = [(0, 0)] * field.ndim
    widths[axis] = (1, 1)
    padded = jnp.pad(field, widths)
    lower = lax.slice_in_dim(padded, 0, count, axis=axis)
    middle = lax.slice_in_dim(padded, 1, count + 1, axis=axis)
    upper = lax.slice_in_dim(padded, 2, count + 2, axis=axis)
    return 0.25 * lower + 0.5 * middle + 0.25 * upper


def smooth_rows(padded, count):
    lower = lax.slice_in_dim(padded, 0, count, axis=2)
    middle = lax.slice_in_dim(padded, 1, count + 1, axis=2)
    upper = lax.slice_in_dim(padded, 2, count + 2, axis=2)
    return 0.25 * lower + 0.5 * middle + 0.25 * upper


def per_device(video, shrink):
    rows_here = video.shape[2]
    values = video.astype(jnp.float32)
    partial_smooth = smooth_local(smooth_local(values, 1), 3)
    extended = padded_2(partial_smooth, (("space", 2),), 1)
    smoothed = smooth_rows(extended, rows_here)
    filtered = (values - smoothed).astype(jnp.bfloat16)
    flattened = filtered.reshape(filtered.shape[0], -1)
    local_gram = jnp.dot(flattened, flattened.T, preferred_element_type=jnp.float32)
    gram_sum = lax.psum(local_gram, "space")
    frames = gram_sum.shape[0]
    ridge = shrink[0] * jnp.trace(gram_sum) / frames
    system = gram_sum + ridge * jnp.eye(frames, dtype=jnp.float32)
    factor = jnp.linalg.cholesky(system)
    inner = lax.linalg.triangular_solve(factor, gram_sum, left_side=True, lower=True)
    mixing = lax.linalg.triangular_solve(
        factor, inner, left_side=True, lower=True, transpose_a=True
    )
    mixing = mixing.astype(jnp.bfloat16)
    result = jnp.dot(mixing.T, flattened, preferred_element_type=jnp.float32)
    return result.astype(jnp.bfloat16).reshape(video.shape)


def solution(mesh):
    return jax.shard_map(
        per_device,
        mesh=mesh,
        in_specs=(P(None, None, ("groups", "space"), None), P("groups")),
        out_specs=P(None, None, ("groups", "space"), None),
        check_vma=False,
    )
```

profile of v0, /device:TPU:0, one launch (start us, length us, event | category | flops | bytes accessed | tf_op | source)
XLA Modules:
  0.0 153.8 jit_solution(1050097050084430542)
XLA Ops:
  0.0 3.3 %copy_convert_fusion = f32[64,16,8,256]{3,1,2,0:T(8,128)S(1)} fusion(bf16[64,16,8,256]{3,2,1,0:T(8,128)(2,1)} %param.2), kind=kLoop, calls=%fused_computation.23 | loop fusion | flops 2097152 | bytes 12582912 | tf_op jit(solution)/shard_map/convert_element_type | solution.py:40
  3.3 5.4 %fusion.2 = f32[64,16,8,256]{3,1,2,0:T(8,128)} fusion(f32[64,16,8,256]{3,1,2,0:T(8,128)S(1)} %copy_convert_fusion), kind=kLoop, calls=%fused_computation.7 | loop fusion | flops 10485760 | bytes 16777216 | tf_op jit(solution)/shard_map/add | solution.py:28
  8.8 0.0 copy-start
  8.8 12.6 %fusion.6 = f32[64,16,8,256]{3,1,2,0:T(8,128)S(1)} fusion(f32[64,16,8,256]{3,1,2,0:T(8,128)} %fusion.2), kind=kLoop, calls=%fused_computation.11 | loop fusion | flops 10485760 | bytes 16777216 | tf_op jit(solution)/shard_map/add | solution.py:28
  21.4 0.2 fusion.24
  21.5 2.4 %collective-permute-start = (f32[64,16,1,256]{3,1,2,0:T(8,128)S(1)}, f32[64,16,1,256]{3,1,2,0:T(8,128)S(1)}, u32[]{:S(2)}, u32[]{:S(2)}) collective-permute-start(f32[64,16,1,256]{3,1,2,0:T(8,128)S(1)} %get-tuple-element.5), channel_id=1, source_target_pairs={{0,1},{1,2},{2,3},{3,4},{4,5},{5,6},{6,7},{7,8},{8,9},{9,10},{10,1... | collective-permute-start | bytes 3145736 | tf_op jit(solution)/shard_map/ppermute | solution.py:14
  24.0 1.3 collective-permute-start.1
  25.9 0.3 collective-permute-done
  26.2 4.4 %collective-permute-done.1 = f32[64,16,1,256]{3,1,2,0:T(8,128)S(1)} collective-permute-done((f32[64,16,1,256]{3,1,2,0:T(8,128)S(1)}, f32[64,16,1,256]{3,1,2,0:T(8,128)S(1)}, u32[]{:S(2)}, u32[]{:S(2)}) %collective-permute-start.1) | collective-permute-done | bytes 1048608 | tf_op jit(solution)/shard_map/ppermute | solution.py:15
  30.6 0.0 copy-done
  30.6 5.9 %fusion.11 = bf16[64,16,8,256]{3,1,2,0:T(8,128)(2,1)} fusion(f32[64,16,1,256]{3,1,2,0:T(8,128)S(1)} %collective-permute-done.1, f32[64,16,8,256]{3,1,2,0:T(8,128)S(1)} %fusion.6, f32[64,16,1,256]{3,1,2,0:T(8,128)S(1)} %collective-permute-done, bf16[64,16,8,256]{3,2,1,0:T(8,128)(2,1)S(1)} %copy-done), kind=kLoop, calls=%fused_computation.17 | loop fusion | flops 20971520 | bytes 18874368 | tf_op jit(solution)/shard_map/convert_element_type | solution.py:44
  36.4 0.0 copy-start.1
  36.4 12.3 %fusion.16 = f32[64,64]{1,0:T(8,128)S(1)} fusion(bf16[64,16,8,256]{3,1,2,0:T(8,128)(2,1)} %fusion.11), kind=kOutput, calls=%fused_computation.24 | convolution fusion | flops 268435456 | bytes 4210688 | tf_op jit(solution)/shard_map/dot_general | solution.py:46
  48.8 0.0 copy-done.1
  48.8 4.2 %copy.14 = bf16[64,16,8,256]{3,2,1,0:T(8,128)(2,1)} copy(bf16[64,16,8,256]{3,1,2,0:T(8,128)(2,1)S(1)} %copy-done.1) | data formatting | bytes 8388608 | tf_op jit(solution)/shard_map/convert_element_type | solution.py:44
  53.0 77.7 %psum.7 = f32[64,64]{1,0:T(8,128)S(1)} all-reduce(f32[64,64]{1,0:T(8,128)S(1)} %fusion.16), channel_id=1, replica_groups=mesh['groups'=2,'space'=16] {'space'}, use_global_device_ids=true, to_apply=%region_0.1 | all-reduce | flops 4096 | bytes 32768 | tf_op jit(solution)/shard_map/psum | solution.py:47
  130.7 0.6 select_reduce_fusion.1
  131.9 0.1 copy.13
  132.0 5.8 %cholesky.17 = f32[64,64]{1,0:T(8,128)S(1)} custom-call(f32[64,64]{1,0:T(8,128)S(1)} %fusion.23), custom_call_target="Cholesky" | custom-call | tf_op jit(solution)/shard_map/jit(cholesky)/cholesky | solution.py:51
  137.9 0.7 compare_reduce_fusion
  138.6 0.7 fusion.19
  139.3 4.9 %custom-call.8 = f32[1,64,64]{1,2,0:T(8,128)S(1)} custom-call(f32[1,64,64]{2,1,0:T(8,128)S(1)} %fusion.19), custom_call_target="InvertDiagBlocksLowerTriangular" | custom-call | tf_op jit(solution)/shard_map/triangular_solve | solution.py:53
  144.2 0.3 fusion.21
  144.5 0.2 convolution_convert_fusion.1
  144.7 4.8 %copy.16 = bf16[8,8,128,256]{3,1,2,0:T(8,128)(2,1)S(1)} copy(bf16[8,8,128,256]{3,2,1,0:T(8,128)(2,1)} %bitcast.27) | data formatting | bytes 8388608
  149.4 1.3 convolution_convert_fusion
  150.7 3.1 %copy.17 = bf16[8,8,128,256]{3,2,1,0:T(8,128)(2,1)} copy(bf16[8,8,128,256]{3,1,2,0:T(8,128)(2,1)S(1)} %bitcast.29) | data formatting | bytes 8388608
  (3 shorter events, 0.1 us)
Async XLA Ops:
  8.8 21.8 %copy-start = (bf16[64,16,8,256]{3,2,1,0:T(8,128)(2,1)S(1)}, bf16[64,16,8,256]{3,2,1,0:T(8,128)(2,1)}, u32[]{:S(2)}) copy-start(bf16[64,16,8,256]{3,2,1,0:T(8,128)(2,1)} %param.2) | copy-start | bytes 12582916
  21.5 4.6 %collective-permute-start = (f32[64,16,1,256]{3,1,2,0:T(8,128)S(1)}, f32[64,16,1,256]{3,1,2,0:T(8,128)S(1)}, u32[]{:S(2)}, u32[]{:S(2)}) collective-permute-start(f32[64,16,1,256]{3,1,2,0:T(8,128)S(1)} %get-tuple-element.5), channel_id=1, source_target_pairs={{0,1},{1,2},{2,3},{3,4},{4,5},{5,6},{6,7},{7,8},{8,9},{9,10},{10,1... | collective-permute-start | bytes 3145736 | tf_op jit(solution)/shard_map/ppermute | solution.py:14
  24.0 6.6 %collective-permute-start.1 = (f32[64,16,1,256]{3,1,2,0:T(8,128)S(1)}, f32[64,16,1,256]{3,1,2,0:T(8,128)S(1)}, u32[]{:S(2)}, u32[]{:S(2)}) collective-permute-start(f32[64,16,1,256]{3,1,2,0:T(8,128)S(1)} %get-tuple-element.6), channel_id=1, source_target_pairs={{1,0},{2,1},{3,2},{4,3},{5,4},{6,5},{7,6},{8,7},{9,8},{10,9},{11,1... | collective-permute-start | bytes 3145736 | tf_op jit(solution)/shard_map/ppermute | solution.py:15
  36.4 12.3 %copy-start.1 = (bf16[64,16,8,256]{3,1,2,0:T(8,128)(2,1)S(1)}, bf16[64,16,8,256]{3,1,2,0:T(8,128)(2,1)}, u32[]{:S(2)}) copy-start(bf16[64,16,8,256]{3,1,2,0:T(8,128)(2,1)} %fusion.11) | copy-start | bytes 12582916
where the time goes:
time: 154 us
  blocking collectives  77.7 us (50%)
  other arithmetic  40 us (26%)
  matrix products  14 us (9%)
  local copies, waits for them, and re-layouts  12.3 us (8%)
  waiting for transfers between devices  4.65 us (3%)
  starting transfers between devices  3.72 us (2%)
    psum x1, blocking collectives, per_device(): gram_sum = lax.psum(local_gram, 'space')  77.7 us
    add x2, other arithmetic, smooth_local(): return 0.25 * lower + 0.5 * middle + 0.25 * upper  18 us
    dot_general x1, matrix products, per_device(): jnp.dot(flattened, flattened.T, preferred_element_type=jnp.float32)  12.3 us
    unnamed x6, local copies, waits for them, and re-layouts  7.86 us
    another operation x3, other arithmetic, per_device(): factor = jnp.linalg.cholesky(system)  6.6 us
    convert_element_type x1, other arithmetic, per_device(): filtered = (values - smoothed).astype(jnp.bfloat16)  5.85 us
    another operation x2, other arithmetic, per_device(): lax.linalg.triangular_solve(factor, inner, left_side=True, lower=True, tr...  5.59 us
    ppermute x1, waiting for transfers between devices, padded_2(): after = lax.ppermute(first, axis, down)  4.39 us
  transfers between devices with their start and end apart: 2, of which 2 were waited for; matrix products, arithmetic and copies ran while one was open for 0% of the time, Pallas kernels for 0%

commit v1 on v0

v1 whole, which is shorter than its diff:
```python
import functools

import jax
import jax.numpy as jnp
from jax import lax
from jax.experimental import pallas as pl
from jax.experimental.pallas import tpu as pltpu
from jax.sharding import PartitionSpec as P

MESH = pl.DeviceIdType.MESH
F32 = jnp.float32
BF16 = jnp.bfloat16


def iota(shape, dim):
    return lax.broadcasted_iota(jnp.int32, shape, dim)


def dot(a, b):
    return jnp.dot(a, b, preferred_element_type=F32)


def chunk_bounds(depth, chunks):
    return [depth * c // chunks for c in range(chunks + 1)]


def filter_kernel(
    cfg, video, flat, gram_out,
    vid, abf, part, send, recv, fbuf, mat, gsend, grecv1, grecv2,
    load_sem, store_sem, hsend_sem, hrecv_sem, g1s_sem, g1r_sem, g2s_sem, g2r_sem,
):
    n, inner, outer, frames, depth, rows, width, block, chunks = cfg
    me = lax.axis_index("space")
    bounds = chunk_bounds(depth, chunks)
    total = frames * rows
    blocks = total // block
    fb = block // rows
    has_prev, has_next = me > 0, me < n - 1

    loads = []
    for c in range(chunks):
        zs = pl.ds(bounds[c], bounds[c + 1] - bounds[c])
        loads.append(pltpu.make_async_copy(video.at[:, zs], vid.at[:, zs], load_sem.at[c]))
        loads[-1].start()

    pos, ring = lax.rem(me, inner), me // inner
    peers1 = [ring * inner + lax.rem(pos + d, inner) for d in range(1, inner)]
    peers2 = [lax.rem(ring + d, outer) * inner + pos for d in range(1, outer)]
    barrier = pltpu.get_barrier_semaphore()

    @pl.when(has_prev)
    def _():
        pl.semaphore_signal(barrier, inc=1, device_id={"space": me - 1}, device_id_type=MESH)

    @pl.when(has_next)
    def _():
        pl.semaphore_signal(barrier, inc=1, device_id={"space": me + 1}, device_id_type=MESH)

    for peer in peers1 + peers2:
        pl.semaphore_signal(barrier, inc=1, device_id={"space": peer}, device_id_type=MESH)

    r, c = iota((block, block), 0), iota((block, block), 1)
    same = (r // rows) == (c // rows)
    step = r - c
    tri = jnp.where(step == 0, 2.0, jnp.where((step == 1) | (step == -1), 1.0, 0.0))
    tri = jnp.where(same, tri, 0.0) / 64.0
    weights = jnp.concatenate([tri, 2.0 * tri, tri], axis=1).astype(BF16)
    r, c = iota((2 * fb, block), 0), iota((2 * fb, block), 1)
    wanted = jnp.where(r < fb, r * rows, (r - fb) * rows + rows - 1)
    pick = jnp.where(wanted == c, 1.0, 0.0).astype(BF16)
    r, c = iota((block, 6 * fb), 0), iota((block, 6 * fb), 1)
    side, zstep = c // (3 * fb), lax.rem(c // fb, 3)
    target = lax.rem(c, fb) * rows + side * (rows - 1)
    hweights = jnp.where(r == target, jnp.where(zstep == 1, 2.0, 1.0), 0.0) / 64.0
    hweights = hweights.astype(BF16)

    zero = jnp.zeros((total, width), BF16)
    abf[0] = zero
    abf[depth + 1] = zero
    for s in range(2):
        recv[s, 0] = jnp.zeros((frames, width), BF16)
        recv[s, depth + 1] = jnp.zeros((frames, width), BF16)

    @pl.when(jnp.logical_not(has_prev))
    def _():
        recv[0] = jnp.zeros((depth + 2, frames, width), BF16)

    @pl.when(jnp.logical_not(has_next))
    def _():
        recv[1] = jnp.zeros((depth + 2, frames, width), BF16)

    def halo(side, c):
        count = bounds[c + 1] - bounds[c]
        return pltpu.make_async_remote_copy(
            src_ref=send.at[side, pl.ds(bounds[c], count)],
            dst_ref=recv.at[side, pl.ds(bounds[c] + 1, count)],
            send_sem=hsend_sem.at[side, c],
            recv_sem=hrecv_sem.at[side, c],
            device_id={"space": me + 1 if side == 0 else me - 1},
            device_id_type=MESH,
        )

    for c in range(chunks):
        loads[c].wait()

        def take(z, carry):
            full = vid[:, z].astype(F32).reshape(total, width).astype(BF16)
            abf[z + 1] = full
            for b in range(blocks):
                ends = dot(pick, full[b * block:(b + 1) * block]).astype(BF16)
                send[1, z, b * fb:(b + 1) * fb] = ends[:fb]
                send[0, z, b * fb:(b + 1) * fb] = ends[fb:]
            return carry

        lax.fori_loop(bounds[c], bounds[c + 1], take, 0)
        if c == 0:
            waits = has_prev.astype(jnp.int32) + has_next.astype(jnp.int32)
            pl.semaphore_wait(barrier, waits + (inner - 1) + (outer - 1))

        @pl.when(has_next)
        def _():
            halo(0, c).start()

        @pl.when(has_prev)
        def _():
            halo(1, c).start()

    def inside(z, carry):
        for b in range(blocks):
            stack = abf[pl.ds(z, 3), b * block:(b + 1) * block].reshape(3 * block, width)
            part[z, b * block:(b + 1) * block] = dot(weights, stack)
        return carry

    lax.fori_loop(0, depth, inside, 0)

    lane = iota((block, width), 1)
    stores = []
    for c in range(chunks):
        @pl.when(has_prev)
        def _():
            halo(0, c).wait_recv()

        @pl.when(has_next)
        def _():
            halo(1, c).wait_recv()

        lo = bounds[c] - 1 if c else 0
        hi = bounds[c + 1] - 1 if c < chunks - 1 else depth

        def finish(z, carry):
            columns = pl.ds(pl.multiple_of(z * width, width), width)
            for b in range(blocks):
                mine = slice(b * block, (b + 1) * block)
                ours = slice(b * fb, (b + 1) * fb)
                above = recv[0, pl.ds(z, 3), ours].reshape(3 * fb, width)
                below = recv[1, pl.ds(z, 3), ours].reshape(3 * fb, width)
                near = part[z, mine] + dot(hweights, jnp.concatenate([above, below], axis=0))
                left = jnp.where(lane == 0, 0.0, pltpu.roll(near, 1, 1))
                right = jnp.where(lane == width - 1, 0.0, pltpu.roll(near, width - 1, 1))
                smooth = (left + right) + 2.0 * near
                fbuf[mine, columns] = (abf[z + 1, mine].astype(F32) - smooth).astype(BF16)
            return carry

        lax.fori_loop(lo, hi, finish, 0)
        cols = pl.ds(lo * width, (hi - lo) * width)
        stores.append(pltpu.make_async_copy(fbuf.at[:, cols], flat.at[:, cols], store_sem.at[c]))
        stores[-1].start()
        for i in range(blocks):
            for j in range(blocks):
                ri, rj = slice(i * block, (i + 1) * block), slice(j * block, (j + 1) * block)
                value = lax.dot_general(
                    fbuf[ri, cols], fbuf[rj, cols], (((1,), (1,)), ((), ())),
                    preferred_element_type=F32,
                )
                mat[ri, rj] = value if c == 0 else mat[ri, rj] + value

    keep = lax.rem(iota((total, total), 0), rows) == lax.rem(iota((total, total), 1), rows)
    kept = jnp.where(keep, mat[...], 0.0)
    summed = jnp.sum(kept.reshape(frames, rows, total), axis=1)
    half = frames // 2
    r, c = iota((total, 2 * frames), 0), iota((total, 2 * frames), 1)
    gather_l = jnp.where(r // rows == c, 1.0, 0.0)
    gather_r = jnp.where(r // rows == c - frames, 1.0, 0.0)
    hp = functools.partial(jnp.dot, preferred_element_type=F32, precision=lax.Precision.HIGHEST)
    packed = hp(summed[:half], gather_l) + hp(summed[half:], gather_r)

    def exchange(value, slot, peers, recv_ref, ssem, rsem):
        gsend[slot] = value
        copies = []
        for d, peer in enumerate(peers):
            copies.append(pltpu.make_async_remote_copy(
                src_ref=gsend.at[slot], dst_ref=recv_ref.at[d],
                send_sem=ssem.at[d], recv_sem=rsem.at[d],
                device_id={"space": peer}, device_id_type=MESH,
            ))
            copies[-1].start()
        for d, copy in enumerate(copies):
            copy.wait_recv()
            value = value + recv_ref[d]
        return value, copies

    packed, copies1 = exchange(packed, 0, peers1, grecv1, g1s_sem, g1r_sem)
    packed, copies2 = exchange(packed, 1, peers2, grecv2, g2s_sem, g2r_sem)
    gram_out[...] = packed
    for copy in copies1 + copies2:
        copy.wait_send()
    for c in range(chunks):
        @pl.when(has_next)
        def _():
            halo(0, c).wait_send()

        @pl.when(has_prev)
        def _():
            halo(1, c).wait_send()
    for store in stores:
        store.wait()


def filtered_gram(video, n):
    frames, depth, rows, width = video.shape
    total = frames * rows
    block = min(total, max(rows, (256 // rows) * rows))
    chunks = 4 if depth % 4 == 0 else 1
    inner = 4 if n % 4 == 0 else (2 if n % 2 == 0 else 1)
    outer = n // inner
    cfg = (n, inner, outer, frames, depth, rows, width, block, chunks)
    half = frames // 2
    dma = pltpu.SemaphoreType.DMA
    return pl.pallas_call(
        functools.partial(filter_kernel, cfg),
        out_shape=(
            jax.ShapeDtypeStruct((total, depth * width), BF16),
            jax.ShapeDtypeStruct((half, 2 * frames), F32),
        ),
        in_specs=[pl.BlockSpec(memory_space=pl.ANY)],
        out_specs=(
            pl.BlockSpec(memory_space=pl.ANY),
            pl.BlockSpec(memory_space=pltpu.VMEM),
        ),
        scratch_shapes=[
            pltpu.VMEM((frames, depth, rows, width), BF16),
            pltpu.VMEM((depth + 2, total, width), BF16),
            pltpu.VMEM((depth, total, width), F32),
            pltpu.VMEM((2, depth, frames, width), BF16),
            pltpu.VMEM((2, depth + 2, frames, width), BF16),
            pltpu.VMEM((total, depth * width), BF16),
            pltpu.VMEM((total, total), F32),
            pltpu.VMEM((2, half, 2 * frames), F32),
            pltpu.VMEM((max(inner - 1, 1), half, 2 * frames), F32),
            pltpu.VMEM((max(outer - 1, 1), half, 2 * frames), F32),
            dma((chunks,)),
            dma((chunks,)),
            dma((2, chunks)),
            dma((2, chunks)),
            dma((max(inner - 1, 1),)),
            dma((max(inner - 1, 1),)),
            dma((max(outer - 1, 1),)),
            dma((max(outer - 1, 1),)),
        ],
        compiler_params=pltpu.CompilerParams(
            collective_id=0, has_side_effects=True, vmem_limit_bytes=48 * 2**20
        ),
    )(video)


def remix_kernel(cfg, shrink, gram, flat, out, fbuf, obuf, load_sem, store_sem):
    frames, depth, rows, width, chunks = cfg
    bounds = chunk_bounds(depth, chunks)
    total, half, lanes = frames * rows, frames // 2, 2 * frames
    loads = []
    for c in range(chunks):
        cols = pl.ds(bounds[c] * width, (bounds[c + 1] - bounds[c]) * width)
        loads.append(pltpu.make_async_copy(flat.at[:, cols], fbuf.at[:, cols], load_sem.at[c]))
        loads[-1].start()

    packed = gram[...]
    other = pltpu.roll(packed, frames, 1)
    r, c = iota((frames, lanes), 0), iota((frames, lanes), 1)
    whole = jnp.where(c < frames, jnp.concatenate([packed, other], axis=0), 0.0)
    eye = jnp.where(r == c, 1.0, 0.0)
    ridge = shrink[0] * jnp.sum(whole * eye) / frames
    system = whole + ridge * eye

    tiles = frames // 8
    parts = [system[8 * t:8 * t + 8] for t in range(tiles)]
    lane, sub = iota((8, lanes), 1), iota((8, lanes), 0)
    for k in range(frames):
        home, at = k // 8, k % 8
        cols = [jnp.broadcast_to(p[:, k:k + 1], (8, lanes)) for p in parts]
        row = jnp.broadcast_to(parts[home][at:at + 1], (8, lanes))
        inverse = 1.0 / jnp.broadcast_to(cols[home][at:at + 1], (8, lanes))
        scaled = row * inverse
        for t in range(tiles):
            new = jnp.where(lane == k, cols[t] * inverse, parts[t] - cols[t] * scaled)
            if t == home:
                new = jnp.where(sub == at, jnp.where(lane == k, -inverse, scaled), new)
            parts[t] = new
    mixing = (eye + ridge * jnp.concatenate(parts, axis=0)).astype(BF16)

    r, c = iota((total, frames), 0), iota((total, frames), 1)
    spread = jnp.where(r // rows == c, 1.0, 0.0).astype(BF16)
    tall = dot(spread, mixing).astype(BF16)
    r, c = iota((lanes, total), 0), iota((lanes, total), 1)
    spread = jnp.where(r == c // rows, 1.0, 0.0).astype(BF16)
    big = dot(tall, spread)
    keep = lax.rem(iota((total, total), 0), rows) == lax.rem(iota((total, total), 1), rows)
    big = jnp.where(keep, big, 0.0).astype(BF16)

    stores = []
    for c in range(chunks):
        loads[c].wait()

        def mix(z, carry):
            columns = pl.ds(pl.multiple_of(z * width, width), width)
            value = dot(big, fbuf[:, columns])
            obuf[:, z] = value.reshape(frames, rows, width).astype(BF16)
            return carry

        lax.fori_loop(bounds[c], bounds[c + 1], mix, 0)
        zs = pl.ds(bounds[c], bounds[c + 1] - bounds[c])
        stores.append(pltpu.make_async_copy(obuf.at[:, zs], out.at[:, zs], store_sem.at[c]))
        stores[-1].start()
    for store in stores:
        store.wait()


def remix(shrink, gram, flat, shape):
    frames, depth, rows, width = shape
    chunks = 4 if depth % 4 == 0 else 1
    cfg = (frames, depth, rows, width, chunks)
    return pl.pallas_call(
        functools.partial(remix_kernel, cfg),
        out_shape=jax.ShapeDtypeStruct(shape, BF16),
        in_specs=[
            pl.BlockSpec(memory_space=pltpu.SMEM),
            pl.BlockSpec(memory_space=pltpu.VMEM),
            pl.BlockSpec(memory_space=pl.ANY),
        ],
        out_specs=pl.BlockSpec(memory_space=pl.ANY),
        scratch_shapes=[
            pltpu.VMEM((frames * rows, depth * width), BF16),
            pltpu.VMEM(shape, BF16),
            pltpu.SemaphoreType.DMA((chunks,)),
            pltpu.SemaphoreType.DMA((chunks,)),
        ],
        compiler_params=pltpu.CompilerParams(vmem_limit_bytes=32 * 2**20),
    )(shrink, gram, flat)


def per_device(n, video, shrink):
    flat, gram = filtered_gram(video, n)
    return remix(shrink, gram, flat, video.shape)


def solution(mesh):
    return jax.shard_map(
        functools.partial(per_device, mesh.shape["space"]),
        mesh=mesh,
        in_specs=(P(None, None, ("groups", "space"), None), P("groups")),
        out_specs=P(None, None, ("groups", "space"), None),
        check_vma=False,
    )
```

time: 154 us -> 50.1 us (0.33)
  blocking collectives: 77.7 us -> 0 us
  Pallas kernels: 0 us -> 49.3 us
  other arithmetic: 40 us -> 0 us
  matrix products: 14 us -> 0 us
  local copies, waits for them, and re-layouts: 12.3 us -> 0 us
  waiting for transfers between devices: 4.65 us -> 0 us
  starting transfers between devices: 3.72 us -> 0 us
    psum x1 -> x0, blocking collectives: 77.7 us -> none  [per_device(): gram_sum = lax.psum(local_gram, 'space')]
    pallas_call x0 -> x2, Pallas kernels: none -> 49.3 us  [the longest x1 33.2 us: filtered_gram(): pl.pallas_call(functools.partial(filter_kernel, cfg), out_shape=(jax.Shap...]
    add x3 -> x0, other arithmetic: 18 us -> none  [the longest x2 18 us: smooth_local(): return 0.25 * lower + 0.5 * middle + 0.25 * upper]
    dot_general x2 -> x0, matrix products: 13.6 us -> none  [the longest x1 12.3 us: per_device(): jnp.dot(flattened, flattened.T, preferred_element_type=jnp.float32)]
    another operation x5 -> x0, other arithmetic: 12.2 us -> none  [the longest x3 6.6 us: per_device(): factor = jnp.linalg.cholesky(system)]
    convert_element_type x2 -> x0, other arithmetic: 9.19 us -> none  [the longest x1 5.85 us: per_device(): filtered = (values - smoothed).astype(jnp.bfloat16)]
    unnamed x6 -> x0, local copies, waits for them, and re-layouts: 7.86 us -> none
    ppermute x2 -> x0, waiting for transfers between devices: 4.65 us -> none  [the longest x1 4.39 us: padded_2(): after = lax.ppermute(first, axis, down)]
  transfers between devices with their start and end apart: 2 -> 0, of which waited for: 2 -> 0; matrix products, arithmetic and copies ran while one was open for 0% -> 0% of each run, Pallas kernels for 0% -> 0%
where the time goes in v1:
time: 50.1 us; the launch traced here: 49.9 us
  Pallas kernels  49.3 us (98%)
  between operations  0.66 us (1%)
    pallas_call x1, Pallas kernels, filtered_gram(): pl.pallas_call(functools.partial(filter_kernel, cfg), out_shape=(jax.Shap...  33.2 us
    pallas_call x1, Pallas kernels, remix(): pl.pallas_call(functools.partial(remix_kernel, cfg), out_shape=jax.ShapeD...  16.1 us

profile of v1, /device:TPU:0, one launch (start us, length us, event | category | flops | bytes accessed | tf_op | source)
XLA Modules:
  0.0 49.9 jit_solution(13579091189501439489)
XLA Ops:
  0.7 33.2 %shard_map.28 = (bf16[512,4096]{1,0:T(8,128)(2,1)S(1)}, f32[32,128]{1,0:T(8,128)S(1)}) custom-call(bf16[64,16,8,256]{3,2,1,0:T(8,128)(2,1)} %video.1), custom_call_target="tpu_custom_call" | custom-call | tf_op jit(solution)/shard_map/pallas_call | solution.py:229
  33.8 16.1 %shard_map.29 = bf16[64,16,8,256]{3,2,1,0:T(8,128)(2,1)} custom-call(f32[1]{0:T(128)S(6)} %copy.3.shrink, f32[32,128]{1,0:T(8,128)S(1)} %get-tuple-element.7.gram, bf16[512,4096]{1,0:T(8,128)(2,1)S(1)} %get-tuple-element.8.flat), custom_call_target="tpu_custom_call" | custom-call | tf_op jit(solution)/shard_map/pallas_call | solution.py:331

commit v2 on v1

v2 whole, which is shorter than its diff:
```python
import functools

import jax
import jax.numpy as jnp
from jax import lax
from jax.experimental import pallas as pl
from jax.experimental.pallas import tpu as pltpu
from jax.sharding import PartitionSpec as P

MESH = pl.DeviceIdType.MESH
F32 = jnp.float32
BF16 = jnp.bfloat16


def iota(shape, dim):
    return lax.broadcasted_iota(jnp.int32, shape, dim)


def dot(a, b):
    return jnp.dot(a, b, preferred_element_type=F32)


def chunk_bounds(depth, chunks):
    return [depth * c // chunks for c in range(chunks + 1)]


def filter_kernel(
    cfg, video, flat, gram_out,
    vid, vox, zsum, recv, acc, gsend, grecv1, grecv2,
    load_sem, hsend_sem, hrecv_sem, g1s_sem, g1r_sem, g2s_sem, g2r_sem,
):
    n, inner, outer, frames, depth, rows, width, block, chunks = cfg
    me = lax.axis_index("space")
    bounds = chunk_bounds(depth, chunks)
    total = frames * rows
    blocks = total // block
    fb = block // rows
    has_prev, has_next = me > 0, me < n - 1

    loads = []
    for c in range(chunks):
        zs = pl.ds(bounds[c], bounds[c + 1] - bounds[c])
        loads.append(pltpu.make_async_copy(video.at[:, zs], vid.at[:, zs], load_sem.at[c]))
        loads[-1].start()

    pos, ring = lax.rem(me, inner), me // inner
    peers1 = [ring * inner + lax.rem(pos + d, inner) for d in range(1, inner)]
    peers2 = [lax.rem(ring + d, outer) * inner + pos for d in range(1, outer)]
    barrier = pltpu.get_barrier_semaphore()

    @pl.when(has_prev)
    def _():
        pl.semaphore_signal(barrier, inc=1, device_id={"space": me - 1}, device_id_type=MESH)

    @pl.when(has_next)
    def _():
        pl.semaphore_signal(barrier, inc=1, device_id={"space": me + 1}, device_id_type=MESH)

    for peer in peers1 + peers2:
        pl.semaphore_signal(barrier, inc=1, device_id={"space": peer}, device_id_type=MESH)

    r, c = iota((block, block), 0), iota((block, block), 1)
    turn = jnp.where(lax.rem(r, fb) * rows + r // fb == c, 1.0, 0.0).astype(BF16)
    r, c = iota((width, width), 0), iota((width, width), 1)
    step = r - c
    along = jnp.where(step == 0, 2.0, jnp.where((step == 1) | (step == -1), 1.0, 0.0))
    along = (along / 64.0).astype(BF16)

    zero = jnp.zeros((frames, width), BF16)
    for y in range(rows):
        vox[y, 0] = zero
        vox[y, depth + 1] = zero
    for s in range(2):
        recv[s, 0] = zero
        recv[s, depth + 1] = zero

    @pl.when(jnp.logical_not(has_prev))
    def _():
        recv[0] = jnp.zeros((depth + 2, frames, width), BF16)

    @pl.when(jnp.logical_not(has_next))
    def _():
        recv[1] = jnp.zeros((depth + 2, frames, width), BF16)

    def halo(side, c):
        zs = pl.ds(bounds[c] + 1, bounds[c + 1] - bounds[c])
        return pltpu.make_async_remote_copy(
            src_ref=vox.at[rows - 1 if side == 0 else 0, zs],
            dst_ref=recv.at[side, zs],
            send_sem=hsend_sem.at[side, c],
            recv_sem=hrecv_sem.at[side, c],
            device_id={"space": me + 1 if side == 0 else me - 1},
            device_id_type=MESH,
        )

    for c in range(chunks):
        loads[c].wait()

        def take(z, carry):
            full = vid[:, z].astype(F32).reshape(total, width).astype(BF16)
            for b in range(blocks):
                turned = dot(turn, full[b * block:(b + 1) * block]).astype(BF16)
                for y in range(rows):
                    vox[y, z + 1, b * fb:(b + 1) * fb] = turned[y * fb:(y + 1) * fb]
            return carry

        lax.fori_loop(bounds[c], bounds[c + 1], take, 0)
        if c == 0:
            waits = has_prev.astype(jnp.int32) + has_next.astype(jnp.int32)
            pl.semaphore_wait(barrier, waits + (inner - 1) + (outer - 1))

        @pl.when(has_next)
        def _():
            halo(0, c).start()

        @pl.when(has_prev)
        def _():
            halo(1, c).start()

    def smooth_xz(field):
        flatter = field.reshape((depth + 2) * frames, width)
        x = dot(flatter, along).reshape(depth + 2, frames, width)
        return (x[:depth] + x[2:]) + 2.0 * x[1:depth + 1]

    def first(y, carry):
        zsum[y] = smooth_xz(vox[y])
        return carry

    lax.fori_loop(0, rows, first, 0)

    def place(slot, y, smooth):
        high = (vox[y, pl.ds(1, depth)].astype(F32) - smooth).astype(BF16)
        base = slot * frames
        if not isinstance(slot, int):
            base = pl.multiple_of(base, frames)
        for z in range(depth):
            flat[pl.ds(base, frames), z * width:(z + 1) * width] = high[z]

    def inside(y, carry):
        place(y - 1, y, (zsum[y - 1] + zsum[y + 1]) + 2.0 * zsum[y])
        return carry

    lax.fori_loop(1, rows - 1, inside, 0)

    def gram_of(pair):
        base = pair * 2 * frames
        if not isinstance(pair, int):
            base = pl.multiple_of(base, 2 * frames)
        both = flat[pl.ds(base, 2 * frames), :]
        return lax.dot_general(
            both, both, (((1,), (1,)), ((), ())), preferred_element_type=F32
        )

    acc[...] = jnp.zeros_like(acc)

    def add_gram(pair, carry):
        acc[...] += gram_of(pair)
        return carry

    lax.fori_loop(0, rows // 2 - 1, add_gram, 0)

    for c in range(chunks):
        @pl.when(has_next)
        def _():
            halo(1, c).wait_recv()
    place(rows - 2, rows - 1, (zsum[rows - 2] + smooth_xz(recv[1])) + 2.0 * zsum[rows - 1])
    for c in range(chunks):
        @pl.when(has_prev)
        def _():
            halo(0, c).wait_recv()
    place(rows - 1, 0, (smooth_xz(recv[0]) + zsum[1]) + 2.0 * zsum[0])

    half = frames // 2
    pairs = acc[...] + gram_of(rows // 2 - 1)
    whole = pairs[:frames] + pltpu.roll(pairs[frames:], frames, 1)
    whole = jnp.where(iota((frames, 2 * frames), 1) < frames, whole, 0.0)
    packed = whole[:half] + pltpu.roll(whole[half:], frames, 1)

    def exchange(value, slot, peers, recv_ref, ssem, rsem):
        gsend[slot] = value
        copies = []
        for d, peer in enumerate(peers):
            copies.append(pltpu.make_async_remote_copy(
                src_ref=gsend.at[slot], dst_ref=recv_ref.at[d],
                send_sem=ssem.at[d], recv_sem=rsem.at[d],
                device_id={"space": peer}, device_id_type=MESH,
            ))
            copies[-1].start()
        for d, copy in enumerate(copies):
            copy.wait_recv()
            value = value + recv_ref[d]
        return value, copies

    packed, copies1 = exchange(packed, 0, peers1, grecv1, g1s_sem, g1r_sem)
    packed, copies2 = exchange(packed, 1, peers2, grecv2, g2s_sem, g2r_sem)
    gram_out[...] = packed
    for copy in copies1 + copies2:
        copy.wait_send()
    for c in range(chunks):
        @pl.when(has_next)
        def _():
            halo(0, c).wait_send()

        @pl.when(has_prev)
        def _():
            halo(1, c).wait_send()


def filtered_gram(video, n):
    frames, depth, rows, width = video.shape
    total = frames * rows
    block = min(total, max(rows, (256 // rows) * rows))
    chunks = 4 if depth % 4 == 0 else 1
    inner = 4 if n % 4 == 0 else (2 if n % 2 == 0 else 1)
    outer = n // inner
    cfg = (n, inner, outer, frames, depth, rows, width, block, chunks)
    half = frames // 2
    dma = pltpu.SemaphoreType.DMA
    return pl.pallas_call(
        functools.partial(filter_kernel, cfg),
        out_shape=(
            jax.ShapeDtypeStruct((total, depth * width), BF16),
            jax.ShapeDtypeStruct((half, 2 * frames), F32),
        ),
        in_specs=[pl.BlockSpec(memory_space=pl.ANY)],
        out_specs=(
            pl.BlockSpec(memory_space=pltpu.VMEM),
            pl.BlockSpec(memory_space=pltpu.VMEM),
        ),
        scratch_shapes=[
            pltpu.VMEM((frames, depth, rows, width), BF16),
            pltpu.VMEM((rows, depth + 2, frames, width), BF16),
            pltpu.VMEM((rows, depth, frames, width), F32),
            pltpu.VMEM((2, depth + 2, frames, width), BF16),
            pltpu.VMEM((2 * frames, 2 * frames), F32),
            pltpu.VMEM((2, half, 2 * frames), F32),
            pltpu.VMEM((max(inner - 1, 1), half, 2 * frames), F32),
            pltpu.VMEM((max(outer - 1, 1), half, 2 * frames), F32),
            dma((chunks,)),
            dma((2, chunks)),
            dma((2, chunks)),
            dma((max(inner - 1, 1),)),
            dma((max(inner - 1, 1),)),
            dma((max(outer - 1, 1),)),
            dma((max(outer - 1, 1),)),
        ],
        compiler_params=pltpu.CompilerParams(
            collective_id=0, has_side_effects=True, vmem_limit_bytes=48 * 2**20
        ),
    )(video)


def remix_kernel(cfg, shrink, gram, flat, out, obuf, store_sem):
    frames, depth, rows, width, chunks = cfg
    bounds = chunk_bounds(depth, chunks)
    total, half, lanes = frames * rows, frames // 2, 2 * frames
    packed = gram[...]
    other = pltpu.roll(packed, frames, 1)
    r, c = iota((frames, lanes), 0), iota((frames, lanes), 1)
    whole = jnp.where(c < frames, jnp.concatenate([packed, other], axis=0), 0.0)
    eye = jnp.where(r == c, 1.0, 0.0)
    ridge = shrink[0] * jnp.sum(whole * eye) / frames
    system = whole + ridge * eye

    tiles = frames // 8
    parts = [system[8 * t:8 * t + 8] for t in range(tiles)]
    lane, sub = iota((8, lanes), 1), iota((8, lanes), 0)
    group = 4
    for k in range(0, frames, group):
        home, at = k // 8, k % 8
        span = range(group)
        cols = [[jnp.broadcast_to(p[:, k + i:k + i + 1], (8, lanes)) for p in parts] for i in span]
        line = [jnp.broadcast_to(parts[home][at + i:at + i + 1], (8, lanes)) for i in span]
        own = {}
        for i in span:
            for j in range(i + 1):
                own[i, j] = jnp.broadcast_to(cols[j][home][at + i:at + i + 1], (8, lanes))

        def of(i, j):
            return own[max(i, j), min(i, j)]

        for q in span:
            inverse = 1.0 / own[q, q]
            scaled = [of(i, q) * inverse for i in span]
            fresh = {}
            for i in span:
                for j in range(i + 1):
                    if i == q and j == q:
                        fresh[i, j] = -inverse
                    elif i == q:
                        fresh[i, j] = scaled[j]
                    elif j == q:
                        fresh[i, j] = scaled[i]
                    else:
                        fresh[i, j] = own[i, j] - of(i, q) * scaled[j]
            own = fresh
        wide = []
        for i in span:
            value = -sum(of(i, j) * line[j] for j in span)
            for j in span:
                value = jnp.where(lane == k + j, of(i, j), value)
            wide.append(value)
        inside = (lane >= k) & (lane < k + group)
        for t in range(tiles):
            terms = [cols[i][t] * wide[i] for i in span]
            while len(terms) > 1:
                terms = [a + b for a, b in zip(terms[::2], terms[1::2])]
            new = jnp.where(inside, 0.0, parts[t]) - terms[0]
            if t == home:
                for i in span:
                    new = jnp.where(sub == at + i, wide[i], new)
            parts[t] = new
    mixing = (eye + ridge * jnp.concatenate(parts, axis=0)).astype(BF16)

    r, c = iota((total, frames), 0), iota((total, frames), 1)
    spread = jnp.where(r // rows == c, 1.0, 0.0).astype(BF16)
    tall = dot(spread, mixing).astype(BF16)
    r, c = iota((lanes, total), 0), iota((lanes, total), 1)
    spread = jnp.where(r == lax.rem(c, frames), 1.0, 0.0).astype(BF16)
    big = dot(tall, spread)
    keep = lax.rem(iota((total, total), 0), rows) == lax.rem(iota((total, total), 1) // frames + 1, rows)
    big = jnp.where(keep, big, 0.0).astype(BF16)

    stores = []
    for c in range(chunks):
        def mix(z, carry):
            columns = pl.ds(pl.multiple_of(z * width, width), width)
            value = dot(big, flat[:, columns])
            obuf[:, z] = value.reshape(frames, rows, width).astype(BF16)
            return carry

        lax.fori_loop(bounds[c], bounds[c + 1], mix, 0)
        zs = pl.ds(bounds[c], bounds[c + 1] - bounds[c])
        stores.append(pltpu.make_async_copy(obuf.at[:, zs], out.at[:, zs], store_sem.at[c]))
        stores[-1].start()
    for store in stores:
        store.wait()


def remix(shrink, gram, flat, shape):
    frames, depth, rows, width = shape
    chunks = 4 if depth % 4 == 0 else 1
    cfg = (frames, depth, rows, width, chunks)
    return pl.pallas_call(
        functools.partial(remix_kernel, cfg),
        out_shape=jax.ShapeDtypeStruct(shape, BF16),
        in_specs=[
            pl.BlockSpec(memory_space=pltpu.SMEM),
            pl.BlockSpec(memory_space=pltpu.VMEM),
            pl.BlockSpec(memory_space=pltpu.VMEM),
        ],
        out_specs=pl.BlockSpec(memory_space=pl.ANY),
        scratch_shapes=[
            pltpu.VMEM(shape, BF16),
            pltpu.SemaphoreType.DMA((chunks,)),
        ],
        compiler_params=pltpu.CompilerParams(vmem_limit_bytes=32 * 2**20),
    )(shrink, gram, flat)


def per_device(n, video, shrink):
    flat, gram = filtered_gram(video, n)
    return remix(shrink, gram, flat, video.shape)


def solution(mesh):
    return jax.shard_map(
        functools.partial(per_device, mesh.shape["space"]),
        mesh=mesh,
        in_specs=(P(None, None, ("groups", "space"), None), P("groups")),
        out_specs=P(None, None, ("groups", "space"), None),
        check_vma=False,
    )
```

time: 50.1 us -> 36.1 us (0.72)
  Pallas kernels: 49.3 us -> 35.3 us
    pallas_call x1, Pallas kernels: 33.2 us -> 25.3 us  [filtered_gram(): pl.pallas_call(functools.partial(filter_kernel, cfg), out_shape=(jax.Shap...]
    pallas_call x1, Pallas kernels: 16.1 us -> 9.94 us  [remix(): pl.pallas_call(functools.partial(remix_kernel, cfg), out_shape=jax.ShapeD...]
where the time goes in v2:
time: 36.1 us; the launch traced here: 35.9 us
  Pallas kernels  35.3 us (98%)
  between operations  0.66 us (2%)
    pallas_call x1, Pallas kernels, filtered_gram(): pl.pallas_call(functools.partial(filter_kernel, cfg), out_shape=(jax.Shap...  25.3 us
    pallas_call x1, Pallas kernels, remix(): pl.pallas_call(functools.partial(remix_kernel, cfg), out_shape=jax.ShapeD...  9.94 us

profile of v2, /device:TPU:0, one launch (start us, length us, event | category | flops | bytes accessed | tf_op | source)
XLA Modules:
  0.0 35.9 jit_solution(8954479995798820882)
XLA Ops:
  0.7 25.3 %shard_map.28 = (bf16[512,4096]{1,0:T(8,128)(2,1)S(1)}, f32[32,128]{1,0:T(8,128)S(1)}) custom-call(bf16[64,16,8,256]{3,2,1,0:T(8,128)(2,1)} %video.1), custom_call_target="tpu_custom_call" | custom-call | tf_op jit(solution)/shard_map/pallas_call | solution.py:219
  26.0 9.9 %shard_map.29 = bf16[64,16,8,256]{3,2,1,0:T(8,128)(2,1)} custom-call(f32[1]{0:T(128)S(6)} %copy.3.shrink, f32[32,128]{1,0:T(8,128)S(1)} %get-tuple-element.7.gram, bf16[512,4096]{1,0:T(8,128)(2,1)S(1)} %get-tuple-element.8.flat), custom_call_target="tpu_custom_call" | custom-call | tf_op jit(solution)/shard_map/pallas_call | solution.py:344

commit v3 on v2

--- a/solution.py
+++ b/solution.py
@@ -14,6 +14,13 @@
 
 def iota(shape, dim):
     return lax.broadcasted_iota(jnp.int32, shape, dim)
+
+
+def recip(x):
+    r = pl.reciprocal(x, approx=True)
+    for _ in range(2):
+        r = r * (2.0 - x * r)
+    return r
 
 
 def dot(a, b):
@@ -96,15 +103,12 @@
     for c in range(chunks):
         loads[c].wait()
 
-        def take(z, carry):
+        for z in range(bounds[c], bounds[c + 1]):
             full = vid[:, z].astype(F32).reshape(total, width).astype(BF16)
             for b in range(blocks):
                 turned = dot(turn, full[b * block:(b + 1) * block]).astype(BF16)
                 for y in range(rows):
                     vox[y, z + 1, b * fb:(b + 1) * fb] = turned[y * fb:(y + 1) * fb]
-            return carry
-
-        lax.fori_loop(bounds[c], bounds[c + 1], take, 0)
         if c == 0:
             waits = has_prev.astype(jnp.int32) + has_next.astype(jnp.int32)
             pl.semaphore_wait(barrier, waits + (inner - 1) + (outer - 1))
@@ -121,12 +125,6 @@
         flatter = field.reshape((depth + 2) * frames, width)
         x = dot(flatter, along).reshape(depth + 2, frames, width)
         return (x[:depth] + x[2:]) + 2.0 * x[1:depth + 1]
-
-    def first(y, carry):
-        zsum[y] = smooth_xz(vox[y])
-        return carry
-
-    lax.fori_loop(0, rows, first, 0)
 
     def place(slot, y, smooth):
         high = (vox[y, pl.ds(1, depth)].astype(F32) - smooth).astype(BF16)
@@ -135,12 +133,6 @@
             base = pl.multiple_of(base, frames)
         for z in range(depth):
             flat[pl.ds(base, frames), z * width:(z + 1) * width] = high[z]
-
-    def inside(y, carry):
-        place(y - 1, y, (zsum[y - 1] + zsum[y + 1]) + 2.0 * zsum[y])
-        return carry
-
-    lax.fori_loop(1, rows - 1, inside, 0)
 
     def gram_of(pair):
         base = pair * 2 * frames
@@ -151,13 +143,14 @@
             both, both, (((1,), (1,)), ((), ())), preferred_element_type=F32
         )
 
-    acc[...] = jnp.zeros_like(acc)
-
-    def add_gram(pair, carry):
-        acc[...] += gram_of(pair)
-        return carry
-
-    lax.fori_loop(0, rows // 2 - 1, add_gram, 0)
+    for y in range(rows):
+        zsum[y] = smooth_xz(vox[y])
+        if y >= 2:
+            place(y - 2, y - 1, (zsum[y - 2] + zsum[y]) + 2.0 * zsum[y - 1])
+    pairs = gram_of(0)
+    for pair in range(1, rows // 2 - 1):
+        pairs = pairs + gram_of(pair)
+    acc[...] = pairs
 
     for c in range(chunks):
         @pl.when(has_next)
@@ -271,16 +264,28 @@
         span = range(group)
         cols = [[jnp.broadcast_to(p[:, k + i:k + i + 1], (8, lanes)) for p in parts] for i in span]
         line = [jnp.broadcast_to(parts[home][at + i:at + i + 1], (8, lanes)) for i in span]
-        own = {}
-        for i in span:
-            for j in range(i + 1):
-                own[i, j] = jnp.broadcast_to(cols[j][home][at + i:at + i + 1], (8, lanes))
+
+        def splats(tile, rows_at, lanes_at):
+            spread = [jnp.broadcast_to(tile[:, j:j + 1], (8, lanes)) for j in lanes_at]
+            return {
+                (i, j): jnp.broadcast_to(spread[j][at_row:at_row + 1], (8, lanes))
+                for i, at_row in enumerate(rows_at) for j in span
+            }
+
+        here = [at + i for i in span]
+        if k == 0:
+            own = splats(parts[home], here, list(span))
+        ahead = k + group
+        if ahead < frames:
+            there = [ahead + j for j in span]
+            old = splats(parts[ahead // 8], [ahead % 8 + i for i in span], there)
+            cross = splats(parts[home], here, there)
 
         def of(i, j):
             return own[max(i, j), min(i, j)]
 
         for q in span:
-            inverse = 1.0 / own[q, q]
+            inverse = recip(own[q, q])
             scaled = [of(i, q) * inverse for i in span]
             fresh = {}
             for i in span:
@@ -300,6 +305,14 @@
             for j in span:
                 value = jnp.where(lane == k + j, of(i, j), value)
             wide.append(value)
+        if ahead < frames:
+            gain = {
+                (i, j): -sum(of(i, m) * cross[m, j] for m in span) for i in span for j in span
+            }
+            following = {
+                (i, j): old[i, j] - sum(cross[m, i] * gain[m, j] for m in span)
+                for i in span for j in range(i + 1)
+            }
         inside = (lane >= k) & (lane < k + group)
         for t in range(tiles):
             terms = [cols[i][t] * wide[i] for i in span]
@@ -310,6 +323,8 @@
                 for i in span:
                     new = jnp.where(sub == at + i, wide[i], new)
             parts[t] = new
+        if ahead < frames:
+            own = following
     mixing = (eye + ridge * jnp.concatenate(parts, axis=0)).astype(BF16)
 
     r, c = iota((total, frames), 0), iota((total, frames), 1)
@@ -323,13 +338,9 @@
 
     stores = []
     for c in range(chunks):
-        def mix(z, carry):
-            columns = pl.ds(pl.multiple_of(z * width, width), width)
-            value = dot(big, flat[:, columns])
+        for z in range(bounds[c], bounds[c + 1]):
+            value = dot(big, flat[:, z * width:(z + 1) * width])
             obuf[:, z] = value.reshape(frames, rows, width).astype(BF16)
-            return carry
-
-        lax.fori_loop(bounds[c], bounds[c + 1], mix, 0)
         zs = pl.ds(bounds[c], bounds[c + 1] - bounds[c])
         stores.append(pltpu.make_async_copy(obuf.at[:, zs], out.at[:, zs], store_sem.at[c]))
         stores[-1].start()

time: 36.1 us -> 32.7 us (0.906)
  Pallas kernels: 35.3 us -> 31.9 us
    pallas_call x1, Pallas kernels: 9.94 us -> 6.74 us  [remix(): pl.pallas_call(functools.partial(remix_kernel, cfg), out_shape=jax.ShapeD...]
where the time goes in v3:
time: 32.7 us; the launch traced here: 32.5 us
  Pallas kernels  31.9 us (98%)
  between operations  0.66 us (2%)
    pallas_call x1, Pallas kernels, filtered_gram(): pl.pallas_call(functools.partial(filter_kernel, cfg), out_shape=(jax.Shap...  25.1 us
    pallas_call x1, Pallas kernels, remix(): pl.pallas_call(functools.partial(remix_kernel, cfg), out_shape=jax.ShapeD...  6.74 us

profile of v3, /device:TPU:0, one launch (start us, length us, event | category | flops | bytes accessed | tf_op | source)
XLA Modules:
  0.0 32.5 jit_solution(1454121178719491275)
XLA Ops:
  0.7 25.1 %shard_map.28 = (bf16[512,4096]{1,0:T(8,128)(2,1)S(1)}, f32[32,128]{1,0:T(8,128)S(1)}) custom-call(bf16[64,16,8,256]{3,2,1,0:T(8,128)(2,1)} %video.1), custom_call_target="tpu_custom_call" | custom-call | tf_op jit(solution)/shard_map/pallas_call | solution.py:212
  25.8 6.7 %shard_map.29 = bf16[64,16,8,256]{3,2,1,0:T(8,128)(2,1)} custom-call(f32[1]{0:T(128)S(6)} %copy.3.shrink, f32[32,128]{1,0:T(8,128)S(1)} %get-tuple-element.7.gram, bf16[512,4096]{1,0:T(8,128)(2,1)S(1)} %get-tuple-element.8.flat), custom_call_target="tpu_custom_call" | custom-call | tf_op jit(solution)/shard_map/pallas_call | solution.py:355

commit v4 on v3

--- a/solution.py
+++ b/solution.py
@@ -122,23 +122,17 @@
             halo(1, c).start()
 
     def smooth_xz(field):
-        flatter = field.reshape((depth + 2) * frames, width)
-        x = dot(flatter, along).reshape(depth + 2, frames, width)
-        return (x[:depth] + x[2:]) + 2.0 * x[1:depth + 1]
-
-    def place(slot, y, smooth):
-        high = (vox[y, pl.ds(1, depth)].astype(F32) - smooth).astype(BF16)
-        base = slot * frames
-        if not isinstance(slot, int):
-            base = pl.multiple_of(base, frames)
-        for z in range(depth):
-            flat[pl.ds(base, frames), z * width:(z + 1) * width] = high[z]
-
-    def gram_of(pair):
-        base = pair * 2 * frames
-        if not isinstance(pair, int):
-            base = pl.multiple_of(base, 2 * frames)
-        both = flat[pl.ds(base, 2 * frames), :]
+        deep = field.shape[0]
+        x = dot(field.reshape(deep * frames, width), along).reshape(deep, frames, width)
+        return (x[:deep - 2] + x[2:]) + 2.0 * x[1:deep - 1]
+
+    def place(slot, y, smooth, lo=0, hi=depth):
+        high = (vox[y, lo + 1:hi + 1].astype(F32) - smooth).astype(BF16)
+        for z in range(lo, hi):
+            flat[slot * frames:(slot + 1) * frames, z * width:(z + 1) * width] = high[z - lo]
+
+    def gram_of(pair, lo=0, hi=depth):
+        both = flat[pair * 2 * frames:(pair + 1) * 2 * frames, lo * width:hi * width]
         return lax.dot_general(
             both, both, (((1,), (1,)), ((), ())), preferred_element_type=F32
         )
@@ -156,15 +150,22 @@
         @pl.when(has_next)
         def _():
             halo(1, c).wait_recv()
-    place(rows - 2, rows - 1, (zsum[rows - 2] + smooth_xz(recv[1])) + 2.0 * zsum[rows - 1])
-    for c in range(chunks):
+
         @pl.when(has_prev)
         def _():
             halo(0, c).wait_recv()
-    place(rows - 1, 0, (smooth_xz(recv[0]) + zsum[1]) + 2.0 * zsum[0])
+
+        lo = bounds[c] - 1 if c else 0
+        hi = bounds[c + 1] - 1 if c < chunks - 1 else depth
+        after = smooth_xz(recv[1, lo:hi + 2])
+        before = smooth_xz(recv[0, lo:hi + 2])
+        last, first = rows - 1, 0
+        place(rows - 2, last, (zsum[last - 1, lo:hi] + after) + 2.0 * zsum[last, lo:hi], lo, hi)
+        place(rows - 1, first, (before + zsum[1, lo:hi]) + 2.0 * zsum[first, lo:hi], lo, hi)
+        acc[...] += gram_of(rows // 2 - 1, lo, hi)
 
     half = frames // 2
-    pairs = acc[...] + gram_of(rows // 2 - 1)
+    pairs = acc[...]
     whole = pairs[:frames] + pltpu.roll(pairs[frames:], frames, 1)
     whole = jnp.where(iota((frames, 2 * frames), 1) < frames, whole, 0.0)
     packed = whole[:half] + pltpu.roll(whole[half:], frames, 1)

time: 32.7 us -> 32.3 us (0.988)
  Pallas kernels: 31.9 us -> 31.5 us
    pallas_call x1, Pallas kernels: 25.1 us -> 24.7 us  [filtered_gram(): pl.pallas_call(functools.partial(filter_kernel, cfg), out_shape=(jax.Shap...]
where the time goes in v4:
time: 32.3 us; the launch traced here: 32.1 us
  Pallas kernels  31.5 us (98%)
  between operations  0.66 us (2%)
    pallas_call x1, Pallas kernels, filtered_gram(): pl.pallas_call(functools.partial(filter_kernel, cfg), out_shape=(jax.Shap...  24.7 us
    pallas_call x1, Pallas kernels, remix(): pl.pallas_call(functools.partial(remix_kernel, cfg), out_shape=jax.ShapeD...  6.74 us

profile of v4, /device:TPU:0, one launch (start us, length us, event | category | flops | bytes accessed | tf_op | source)
XLA Modules:
  0.0 32.1 jit_solution(6001357278219906462)
XLA Ops:
  0.7 24.7 %shard_map.28 = (bf16[512,4096]{1,0:T(8,128)(2,1)S(1)}, f32[32,128]{1,0:T(8,128)S(1)}) custom-call(bf16[64,16,8,256]{3,2,1,0:T(8,128)(2,1)} %video.1), custom_call_target="tpu_custom_call" | custom-call | tf_op jit(solution)/shard_map/pallas_call | solution.py:213
  25.4 6.7 %shard_map.29 = bf16[64,16,8,256]{3,2,1,0:T(8,128)(2,1)} custom-call(f32[1]{0:T(128)S(6)} %copy.3.shrink, f32[32,128]{1,0:T(8,128)S(1)} %get-tuple-element.7.gram, bf16[512,4096]{1,0:T(8,128)(2,1)S(1)} %get-tuple-element.8.flat), custom_call_target="tpu_custom_call" | custom-call | tf_op jit(solution)/shard_map/pallas_call | solution.py:356
